TPU v7x, 32 devices: a whole 2x2x4 slice. The times are simulated.
32 devices in a mesh: samples: 4 (over y, x), space: 8 (over z, core).
Axes of the slice: x: 2, y: 2, z: 4, core: 2. Of those that a mesh axis runs over, the one named last changes fastest.
Arguments:
- target: bfloat16 [8, 8192, 4096], P(None, 'samples', 'space'), may hold values from 0 to 1
- a_factor: bfloat16 [8192, 256], P(('samples', 'space')), may hold values from -3 to 3
- b_factor: bfloat16 [4096, 256], P(('space', 'samples')), may hold values from -3 to 3
- c_factor: bfloat16 [8, 256], replicated, may hold values from -3 to 3
Outputs:
- grad_a: float32 [8192, 256], P(('samples', 'space'))
- grad_b: float32 [4096, 256], P(('space', 'samples'))
- grad_c: float32 [8, 256], replicated
All inputs are finite; a program needn't handle non-finite values.
Results may differ from a plain program's by a relative error of at most 0.002.
Values may be sent and summed in bfloat16 or wider, within the bound.
A program may use at most 128 MiB of HBM per device.

v0:
```python
import jax
import jax.numpy as jnp
from jax import lax
from jax.sharding import PartitionSpec as P


def on_device(target, a_factor, b_factor, c_factor):
    a_full = lax.all_gather(a_factor, "space", axis=0, tiled=True)
    b_full = lax.all_gather(b_factor, "samples", axis=0, tiled=True)
    c_wide = c_factor.astype(jnp.float32)
    scaled = (c_wide[:, None, :] * a_full.astype(jnp.float32)[None]).astype(jnp.bfloat16)
    model = jnp.einsum("kir,jr->kij", scaled, b_full, preferred_element_type=jnp.float32)
    derivative = (jax.nn.sigmoid(model) - target.astype(jnp.float32)).astype(jnp.bfloat16)
    weighted = jnp.einsum("kij,ir->kjr", derivative, a_full, preferred_element_type=jnp.float32)
    b_part = jnp.sum(weighted * c_wide[:, None, :], axis=0)
    c_part = jnp.sum(weighted * b_full.astype(jnp.float32)[None], axis=1)
    own_a = a_factor.shape[0]
    own_b = b_factor.shape[0]
    inner = jnp.einsum("kij,jr->kir", derivative, b_full, preferred_element_type=jnp.float32)
    whole_a = lax.psum(jnp.sum(inner * c_wide[:, None, :], axis=0), "space")
    grad_a = lax.dynamic_slice_in_dim(whole_a, lax.axis_index("space") * own_a, own_a, 0)
    whole_b = lax.psum(b_part, "samples")
    grad_b = lax.dynamic_slice_in_dim(whole_b, lax.axis_index("samples") * own_b, own_b, 0)
    grad_c = lax.psum(c_part, ("samples", "space"))
    return (grad_a, grad_b, grad_c)


def solution(mesh):
    return jax.shard_map(
        on_device,
        mesh=mesh,
        in_specs=(
            P(None, "samples", "space"),
            P(("samples", "space"), None),
            P(("space", "samples"), None),
            P(),
        ),
        out_specs=(P(("samples", "space"), None), P(("space", "samples"), None), P()),
        check_vma=False,
    )
```

profile of v0, /device:TPU:0, one launch (start us, length us, event | category | flops | bytes accessed | tf_op | source)
XLA Modules:
  0.0 185.7 jit_solution(16198696957152597542)
XLA Ops:
  7.2 0.0 all-gather.2.cloned.1.call-start
  7.2 0.7 all-gather.2.cloned.1.call-update
  7.9 0.0 all-reduce.5.cloned.1.call-start
  7.9 0.7 convert_element_type.18
  8.6 10.7 %all_gather.7 = bf16[512,256]{1,0:T(8,128)(2,1)S(1)} all-gather(bf16[128,256]{1,0:T(8,128)(2,1)} %param.6), channel_id=1, replica_groups=mesh['samples'=4,'space'=8] {'samples'}, dimensions={0}, use_global_device_ids=true | all-gather | bytes 327680 | tf_op jit(solution)/shard_map/all_gather | solution.py:9
  19.4 15.0 %all-gather.2.cloned.1.call-done = bf16[2048,256]{1,0:T(8,128)(2,1)} async-done(((bf16[256,256]{1,0:T(8,128)(2,1)}), bf16[2048,256]{1,0:T(8,128)(2,1)}) %all-gather.2.cloned.1.call-update) | async-done | bytes 1048592 | tf_op jit(solution)/shard_map/all_gather | solution.py:8
  34.4 1.4 convert_element_type.19
  35.8 0.0 copy-start
  35.8 17.1 %subtract_convert_fusion = bf16[8,2048,512]{2,1,0:T(8,128)(2,1)} fusion(bf16[8,2048,512]{2,1,0:T(8,128)(2,1)} %param.4, f32[2048,256]{1,0:T(8,128)S(1)} %convert_element_type.19, f32[8,256]{1,0:T(8,128)S(1)} %convert_element_type.18, bf16[512,256]{1,0:T(8,128)(2,1)S(1)} %all_gather.7), kind=kOutput, calls=%fused_computation | convolution fusion | flops 4353687552 | bytes 35921920 | tf_op jit(solution)/shard_map/kir,jr->kij/dot_general | solution.py:12
  52.9 0.0 copy-done
  52.9 11.7 %multiply_reduce_fusion.1 = (f32[8,256]{1,0:T(8,128)S(1)}, f32[512,256]{1,0:T(8,128)}) fusion(f32[512,256]{1,0:T(8,128)S(1)} %convert_element_type.23, f32[8,256]{1,0:T(8,128)S(1)} %convert_element_type.18, bf16[8,2048,512]{2,1,0:T(8,128)(2,1)} %subtract_convert_fusion, bf16[2048,256]{1,0:T(8,128)(2,1)S(1)} %copy-done), kind=kOutput, calls=%fused_computation.5 | convolution fusion | flops 4299028480 | bytes 18890752 | tf_op jit(solution)/shard_map/kij,ir->kjr/dot_general | solution.py:14
  64.6 0.0 all-reduce.5.cloned.1.call-update
  64.6 0.2 all-reduce.3.cloned.1.call-start
  64.9 12.0 %multiply_reduce_fusion = f32[2048,256]{1,0:T(8,128)} fusion(f32[8,256]{1,0:T(8,128)S(1)} %convert_element_type.18, bf16[8,2048,512]{2,1,0:T(8,128)(2,1)} %subtract_convert_fusion, bf16[512,256]{1,0:T(8,128)(2,1)S(1)} %all_gather.7), kind=kOutput, calls=%fused_computation.1 | convolution fusion | flops 4302831616 | bytes 19144704 | tf_op jit(solution)/shard_map/kij,jr->kir/dot_general | solution.py:19
  76.9 0.0 all-reduce.3.cloned.1.call-update
  76.9 40.4 %psum.23 = f32[8,256]{1,0:T(8,128)} all-reduce(f32[8,256]{1,0:T(8,128)S(1)} %get-tuple-element.3), channel_id=1, replica_groups=mesh['samples'=4,'space'=8] {'samples','space'}, use_global_device_ids=true, to_apply=%region_5.0 | all-reduce | flops 2048 | bytes 16384 | tf_op jit(solution)/shard_map/psum | solution.py:24
  117.3 0.0 all-reduce.5.cloned.1.call-done
  117.3 1.6 constant_dynamic-slice_fusion
  118.9 58.6 %all-reduce.3.cloned.1.call-done = f32[2048,256]{1,0:T(8,128)} async-done(((f32[2048,256]{1,0:T(8,128)}), f32[2048,256]{1,0:T(8,128)}) %all-reduce.3.cloned.1.call-update) | async-done | bytes 2097168 | tf_op jit(solution)/shard_map/psum | solution.py:20
  177.5 1.7 constant_dynamic-slice_fusion.1
  (1 shorter events, 0.0 us)
Async XLA Ops:
  7.2 27.3 %all-gather.2.cloned.1.call-start = ((), (), s32[]{:S(2)}) async-start(), calls=%async_computation | async-start | bytes 1179648 | tf_op jit(solution)/shard_map/all_gather | solution.py:8
  7.9 109.4 %all-reduce.5.cloned.1.call-start = ((), (), s32[]{:S(2)}) async-start(), calls=%async_computation.2 | async-start | bytes 1048576 | tf_op jit(solution)/shard_map/psum | solution.py:22
  35.8 17.1 %copy-start = (bf16[2048,256]{1,0:T(8,128)(2,1)S(1)}, bf16[2048,256]{1,0:T(8,128)(2,1)}, u32[]{:S(2)}) copy-start(bf16[2048,256]{1,0:T(8,128)(2,1)} %all-gather.2.cloned.1.call-done) | copy-start | bytes 3145732
  64.6 112.8 %all-reduce.3.cloned.1.call-start = ((), (), s32[]{:S(2)}) async-start(), calls=%async_computation.1 | async-start | bytes 4194304 | tf_op jit(solution)/shard_map/psum | solution.py:20
Sparse Core Ops, SparseCore 0:
  9.6 24.7 all-gather.1
  64.8 45.2 all-reduce.4
  112.5 64.9 all-reduce.2
where the time goes:
time: 186 us
  waiting for transfers between devices  74.4 us (40%)
  blocking collectives  51.1 us (27%)
  matrix products  40.8 us (22%)
  between operations  13.8 us (7%)
  local copies, waits for them, and re-layouts  3.26 us (2%)
  other arithmetic  2.11 us (1%)
    psum x1, waiting for transfers between devices, on_device(): whole_a = lax.psum(jnp.sum(inner * c_wide[:, None, :], axis=0), 'space')  58.6 us
    psum x1, blocking collectives, on_device(): grad_c = lax.psum(c_part, ('samples', 'space'))  40.4 us
    dot_general x1, matrix products, on_device(): jnp.einsum('kir,jr->kij', scaled, b_full, preferred_element_type=jnp.floa...  17.1 us
    all_gather x1, waiting for transfers between devices, on_device(): a_full = lax.all_gather(a_factor, 'space', axis=0, tiled=True)  15 us
    dot_general x1, matrix products, on_device(): jnp.einsum('kij,jr->kir', derivative, b_full, preferred_element_type=jnp....  12 us
    dot_general x1, matrix products, on_device(): jnp.einsum('kij,ir->kjr', derivative, a_full, preferred_element_type=jnp....  11.7 us
    all_gather x1, blocking collectives, on_device(): b_full = lax.all_gather(b_factor, 'samples', axis=0, tiled=True)  10.7 us
  transfers between devices with their start and end apart: 3, of which 2 were waited for; matrix products, arithmetic and copies ran while one was open for 8% of the time, Pallas kernels for 0%

commit v1 on v0

v1 whole, which is shorter than its diff:
```python
import functools

import jax
import jax.numpy as jnp
from jax import lax
from jax.experimental import pallas as pl
from jax.experimental.pallas import tpu as pltpu
from jax.sharding import PartitionSpec as P

MESH = pl.DeviceIdType.MESH
F32 = jnp.float32
BF16 = jnp.bfloat16
GROUP = 4


def matmul(x, y):
    return jnp.dot(x, y, preferred_element_type=F32)


def kernel(
    n_samples, n_space,
    target, a_own, b_own, c_ref,
    grad_a, grad_b, grad_c,
    t_buf, a_buf, b_buf, b_turned, c_down, c_along,
    d_buf0, d_buf1, s_buf0, s_buf1,
    sum_b, sum_c, part, sib_part, z_out, z_in, b_out, b_in, c_in, c_all,
    t_sem, a_recv, b_recv, b_send, a_send, fwd_send,
    sib_send, sib_recv, z_send, z_recv, gb_send, gb_recv,
    gc_send, gc_recv, gd_send, gd_recv,
):
    steps, width = c_ref.shape
    own_a = a_own.shape[0]
    own_b = b_own.shape[0]
    chips = n_space // 2
    m = lax.axis_index("samples")
    s = lax.axis_index("space")
    z, core = lax.div(s, 2), lax.rem(s, 2)
    sibling = z * 2 + 1 - core

    def other(d):
        found, bit = 0, 1
        while bit < chips:
            found = found + bit * lax.rem(lax.div(z, bit) + lax.div(jnp.int32(d), bit), 2)
            bit *= 2
        return found

    def block_at(t):
        pair, half = lax.div(t, 2), lax.rem(t, 2)
        flip = lax.div(pair + 1, chips)
        return other(lax.rem(pair + 1, chips)) * 2 + lax.rem(core + half + flip, 2)

    def load(t):
        rows = pl.ds(pl.multiple_of(block_at(t) * own_a, own_a), own_a)
        return pltpu.make_async_copy(target.at[:, rows, :], t_buf.at[t], t_sem.at[t])

    def send(src, dst, send_sem, recv_sem, **where):
        return pltpu.make_async_remote_copy(
            src_ref=src, dst_ref=dst, send_sem=send_sem, recv_sem=recv_sem,
            device_id=where, device_id_type=MESH,
        )

    def arrived(buf, sem):
        pltpu.make_async_copy(buf, buf, sem).wait()

    def send_b(i):
        return send(b_own, b_buf.at[m], b_send.at[i], b_recv.at[m], samples=lax.rem(m + i, n_samples))

    def send_a(d):
        to = sibling if d == 0 else other(d) * 2 + core
        return send(a_own, a_buf.at[s], a_send.at[d], a_recv.at[s], space=to)

    def send_far(d):
        return send(a_own, a_buf.at[s], a_send.at[d], a_recv.at[s], space=other(d) * 2 + core)

    def forward(t):
        block = a_buf.at[block_at(t)]
        return send(block, block, fwd_send.at[lax.div(t, 2)], a_recv.at[block_at(t)], space=sibling)

    def to_sibling(t, pair):
        return send(part.at[t], sib_part.at[pair], sib_send.at[pair], sib_recv.at[pair], space=sibling)

    def to_owner(pair):
        return send(
            z_out.at[pair], z_in.at[pair], z_send.at[pair], z_recv.at[pair],
            space=other(pair + 1) * 2 + core,
        )

    def send_gb(i):
        to = lax.rem(m + i, n_samples)
        return send(b_out.at[to], b_in.at[m], gb_send.at[i], gb_recv.at[m], samples=to)

    def send_gc(i):
        return send(c_in.at[m], c_in.at[m], gc_send.at[i], gc_recv.at[m], samples=lax.rem(m + i, n_samples))

    def send_gd(i):
        return send(c_all.at[s], c_all.at[s], gd_send.at[i], gd_recv.at[s], space=lax.rem(s + i, n_space))

    barrier = pltpu.get_barrier_semaphore()
    for i in range(1, n_samples):
        pl.semaphore_signal(barrier, inc=1, device_id={"samples": lax.rem(m + i, n_samples)}, device_id_type=MESH)
    for i in range(1, n_space):
        pl.semaphore_signal(barrier, inc=1, device_id={"space": lax.rem(s + i, n_space)}, device_id_type=MESH)
    own_b_copy = pltpu.make_async_copy(b_own, b_buf.at[m], b_recv.at[m])
    own_b_copy.start()
    own_a_copy = pltpu.make_async_copy(a_own, a_buf.at[s], a_recv.at[s])
    own_a_copy.start()
    load(jnp.int32(0)).start()
    pl.semaphore_wait(barrier, n_samples + n_space - 2)

    for i in range(1, n_samples):
        send_b(i).start()
    send_a(1).start()
    send_a(0).start()

    def start_load(t, carry):
        load(t).start()
        return carry

    lax.fori_loop(1, n_space, start_load, 0)

    c_wide = c_ref[...].astype(F32)
    c_turned = c_wide.T
    for k in range(steps):
        c_along[k] = jnp.broadcast_to(c_wide[k:k + 1, :], (own_a, width)).astype(BF16)
        c_down[k] = jnp.broadcast_to(c_turned[:, k:k + 1], (width, own_a)).astype(BF16)
    sum_b[...] = jnp.zeros_like(sum_b)
    sum_c[...] = jnp.zeros_like(sum_c)

    def wait_b(i, carry):
        arrived(b_buf.at[i], b_recv.at[i])
        return carry

    lax.fori_loop(0, n_samples, wait_b, 0)
    if chips > 2:
        send_a(2).start()
    b_all = b_buf[...].reshape(n_samples * own_b, width)
    b_turned[...] = (b_all.astype(F32) * 0.5).T.astype(BF16)

    def step(t, carry):
        pair = lax.div(t, 2)
        even = lax.rem(t, 2) == 0
        block = block_at(t)
        arrived(a_buf.at[block], a_recv.at[block])

        @pl.when(jnp.logical_and(even, t < n_space - 2))
        def _():
            forward(t).start()

        @pl.when(jnp.logical_and(even, pair + 3 < chips))
        def _():
            send_far(pair + 3).start()

        load(t).wait()
        a = a_buf[block]
        a_wide = a.astype(F32)
        a_turned = a_wide.T.astype(BF16)
        b_full = b_buf[...].reshape(n_samples * own_b, width)
        total = jnp.zeros((own_a, width), F32)
        for g, (d_buf, s_buf) in enumerate(((d_buf0, s_buf0), (d_buf1, s_buf1))):
            for j in range(GROUP):
                k = g * GROUP + j
                rows = slice(j * own_a, (j + 1) * own_a)
                half_model = matmul(a * c_along[k], b_turned[...])
                derivative = (0.5 * jnp.tanh(half_model) + (0.5 - t_buf[t, k].astype(F32))).astype(BF16)
                d_buf[rows, :] = derivative
                s_buf[:, rows] = a_turned * c_down[k]
                inner = matmul(derivative, b_full)
                total = total + inner * c_ref[k:k + 1, :].astype(F32)
                sum_c[k] += jnp.sum((a_wide * inner).reshape(own_a // 8, 8, width), axis=0)
            sum_b[...] += matmul(s_buf[...], d_buf[...])
        part[t] = total

        last = t == n_space - 2

        @pl.when(jnp.logical_or(last, jnp.logical_and(jnp.logical_not(even), t < n_space - 2)))
        def _():
            to_sibling(t, pair).start()

        @pl.when(jnp.logical_and(even, t >= 2))
        def _():
            before = pair - 1
            arrived(sib_part.at[before], sib_recv.at[before])
            z_out[before] = (part[t - 2] + sib_part[before]).astype(BF16)
            to_owner(before).start()

        return carry

    lax.fori_loop(0, n_space, step, 0)

    for k in range(steps):
        c_in[m, pl.ds(k, 1), :] = jnp.sum(sum_c[k], axis=0, keepdims=True)
    for i in range(1, n_samples):
        send_gc(i).start()
    turned = sum_b[...].T
    b_out[...] = turned.astype(BF16).reshape(n_samples, own_b, width)
    for i in range(1, n_samples):
        send_gb(i).start()

    arrived(sib_part.at[chips - 1], sib_recv.at[chips - 1])
    total = part[n_space - 1] + sib_part[chips - 1]
    for pair in range(chips - 1):
        arrived(z_in.at[pair], z_recv.at[pair])
        total = total + z_in[pair].astype(F32)
    grad_a[...] = total

    for i in range(1, n_samples):
        came = lax.rem(m + i, n_samples)
        arrived(c_in.at[came], gc_recv.at[came])
    c_all[s] = jnp.sum(c_in[...], axis=0)
    for i in range(1, n_space):
        send_gd(i).start()

    total = b_out[m].astype(F32)
    for i in range(1, n_samples):
        came = lax.rem(m + i, n_samples)
        arrived(b_in.at[came], gb_recv.at[came])
        total = total + b_in[came].astype(F32)
    grad_b[...] = total

    for i in range(1, n_space):
        came = lax.rem(s + i, n_space)
        arrived(c_all.at[came], gd_recv.at[came])
    grad_c[...] = jnp.sum(c_all[...], axis=0)

    for i in range(1, n_samples):
        send_b(i).wait_send()
        send_gb(i).wait_send()
        send_gc(i).wait_send()
    for d in range(chips):
        send_a(d).wait_send()
    for pair in range(chips - 1):
        forward(jnp.int32(2 * pair)).wait_send()
        to_owner(pair).wait_send()
        to_sibling(2 * pair + 1, pair).wait_send()
    to_sibling(n_space - 2, chips - 1).wait_send()
    for i in range(1, n_space):
        send_gd(i).wait_send()


def on_device(n_samples, n_space, target, a_factor, b_factor, c_factor):
    steps, rows, columns = target.shape
    own_a, width = a_factor.shape
    own_b = b_factor.shape[0]
    chips = n_space // 2
    vmem, dma = pltpu.VMEM, pltpu.SemaphoreType.DMA
    flops = 6 * steps * rows * columns * width
    anywhere = pl.BlockSpec(memory_space=pl.ANY)
    inside = pl.BlockSpec(memory_space=pltpu.VMEM)
    return pl.pallas_call(
        functools.partial(kernel, n_samples, n_space),
        out_shape=(
            jax.ShapeDtypeStruct((own_a, width), F32),
            jax.ShapeDtypeStruct((own_b, width), F32),
            jax.ShapeDtypeStruct((steps, width), F32),
        ),
        in_specs=[anywhere, anywhere, anywhere, inside],
        out_specs=(inside, inside, inside),
        scratch_shapes=[
            vmem((n_space, steps, own_a, columns), BF16),
            vmem((n_space, own_a, width), BF16),
            vmem((n_samples, own_b, width), BF16),
            vmem((width, columns), BF16),
            vmem((steps, width, own_a), BF16),
            vmem((steps, own_a, width), BF16),
            vmem((GROUP * own_a, columns), BF16),
            vmem((GROUP * own_a, columns), BF16),
            vmem((width, GROUP * own_a), BF16),
            vmem((width, GROUP * own_a), BF16),
            vmem((width, columns), F32),
            vmem((steps, 8, width), F32),
            vmem((n_space, own_a, width), F32),
            vmem((chips, own_a, width), F32),
            vmem((chips, own_a, width), BF16),
            vmem((chips, own_a, width), BF16),
            vmem((n_samples, own_b, width), BF16),
            vmem((n_samples, own_b, width), BF16),
            vmem((n_samples, steps, width), F32),
            vmem((n_space, steps, width), F32),
            dma((n_space,)), dma((n_space,)), dma((n_samples,)), dma((n_samples,)),
            dma((chips,)), dma((chips,)),
            dma((chips,)), dma((chips,)), dma((chips,)), dma((chips,)),
            dma((n_samples,)), dma((n_samples,)),
            dma((n_samples,)), dma((n_samples,)),
            dma((n_space,)), dma((n_space,)),
        ],
        compiler_params=pltpu.CompilerParams(
            collective_id=0, has_side_effects=True, vmem_limit_bytes=56 * 1024 * 1024
        ),
        cost_estimate=pl.CostEstimate(
            flops=flops, bytes_accessed=target.size * 2, transcendentals=target.size
        ),
        name="cp_gradient",
    )(target, a_factor, b_factor, c_factor)


def solution(mesh):
    n_samples, n_space = mesh.shape["samples"], mesh.shape["space"]
    return jax.shard_map(
        functools.partial(on_device, n_samples, n_space),
        mesh=mesh,
        in_specs=(
            P(None, "samples", "space"),
            P(("samples", "space"), None),
            P(("space", "samples"), None),
            P(),
        ),
        out_specs=(P(("samples", "space"), None), P(("space", "samples"), None), P()),
        check_vma=False,
    )
```

time: 186 us -> 48.7 us (0.26)
  waiting for transfers between devices: 74.4 us -> 0 us
  blocking collectives: 51.1 us -> 0 us
  Pallas kernels: 0 us -> 43.2 us
  matrix products: 40.8 us -> 0 us
  between operations: 13.8 us -> 0.64 us
  other arithmetic: 2.11 us -> 0 us
    psum x2 -> x0, waiting for transfers between devices: 58.6 us -> none  [the longest x1 58.6 us: on_device(): whole_a = lax.psum(jnp.sum(inner * c_wide[:, None, :], axis=0), 'space')]
    pallas_call x0 -> x1, Pallas kernels: none -> 43.2 us  [on_device(): pl.pallas_call(functools.partial(kernel, n_samples, n_space), out_shape=(...]
    dot_general x3 -> x0, matrix products: 40.8 us -> none  [the longest x1 17.1 us: on_device(): jnp.einsum('kir,jr->kij', scaled, b_full, preferred_element_type=jnp.floa...]
    psum x1 -> x0, blocking collectives: 40.4 us -> none  [on_device(): grad_c = lax.psum(c_part, ('samples', 'space'))]
    all_gather x1 -> x0, waiting for transfers between devices: 15 us -> none  [on_device(): a_full = lax.all_gather(a_factor, 'space', axis=0, tiled=True)]
    all_gather x1 -> x0, blocking collectives: 10.7 us -> none  [on_device(): b_full = lax.all_gather(b_factor, 'samples', axis=0, tiled=True)]
    unnamed x2 -> x3, local copies, waits for them, and re-layouts: 0.01 us -> 4.53 us
    dynamic_slice x2 -> x0, local copies, waits for them, and re-layouts: 3.25 us -> none  [the longest x1 1.67 us: on_device(): lax.dynamic_slice_in_dim(whole_a, lax.axis_index('space') * own_a, own_a, 0)]
  transfers between devices with their start and end apart: 3 -> 0, of which waited for: 2 -> 0; matrix products, arithmetic and copies ran while one was open for 8% -> 0% of each run, Pallas kernels for 0% -> 0%
where the time goes in v1:
time: 48.7 us; the launch traced here: 48.4 us
  Pallas kernels  43.2 us (89%)
  local copies, waits for them, and re-layouts  4.53 us (9%)
  between operations  0.64 us (1%)
    pallas_call x1, Pallas kernels, on_device(): pl.pallas_call(functools.partial(kernel, n_samples, n_space), out_shape=(...  43.2 us
    unnamed x3, local copies, waits for them, and re-layouts  4.53 us

profile of v1, /device:TPU:0, one launch (start us, length us, event | category | flops | bytes accessed | tf_op | source)
XLA Modules:
  0.0 48.4 jit_solution(9751136238573771125)
XLA Ops:
  0.6 43.2 %cp_gradient.1 = (f32[256,256]{1,0:T(8,128)}, f32[128,256]{1,0:T(8,128)}, f32[8,256]{1,0:T(8,128)}) custom-call(bf16[8,2048,512]{2,1,0:T(8,128)(2,1)} %target.1, bf16[256,256]{1,0:T(8,128)(2,1)} %a_own.1, bf16[128,256]{1,0:T(8,128)(2,1)} %b_own.1, bf16[8,256]{1,0:T(8,128)(2,1)} %c_ref.1), custom_call_target="tpu_custom_call" | custom-call | flops 12884901888 | bytes 16777216 | tf_op jit(solution)/shard_map/cp_gradient/pallas_call | solution.py:249
  43.9 1.7 %copy.10 = f32[256,256]{1,0:T(8,128)} copy(f32[256,256]{1,0:T(8,128)} %get-tuple-element.6) | data formatting | bytes 524288
  45.6 1.6 %copy.11 = f32[128,256]{1,0:T(8,128)} copy(f32[128,256]{1,0:T(8,128)} %get-tuple-element.7) | data formatting | bytes 262144
  47.1 1.3 %copy.12 = f32[8,256]{1,0:T(8,128)} copy(f32[8,256]{1,0:T(8,128)} %get-tuple-element.8) | data formatting | bytes 16384

commit v2 on v1

--- a/solution.py
+++ b/solution.py
@@ -11,6 +11,7 @@
 F32 = jnp.float32
 BF16 = jnp.bfloat16
 GROUP = 4
+CHUNK = 32
 
 
 def matmul(x, y):
@@ -21,8 +22,8 @@
     n_samples, n_space,
     target, a_own, b_own, c_ref,
     grad_a, grad_b, grad_c,
-    t_buf, a_buf, b_buf, b_turned, c_down, c_along,
-    d_buf0, d_buf1, s_buf0, s_buf1,
+    t_buf, a_buf, b_buf, b_half, b_turned, c_down, c_along,
+    h_bufs, d_bufs, s_bufs, x_buf, inner_buf, a_turned, a_before,
     sum_b, sum_c, part, sib_part, z_out, z_in, b_out, b_in, c_in, c_all,
     t_sem, a_recv, b_recv, b_send, a_send, fwd_send,
     sib_send, sib_recv, z_send, z_recv, gb_send, gb_recv,
@@ -122,7 +123,7 @@
     c_turned = c_wide.T
     for k in range(steps):
         c_along[k] = jnp.broadcast_to(c_wide[k:k + 1, :], (own_a, width)).astype(BF16)
-        c_down[k] = jnp.broadcast_to(c_turned[:, k:k + 1], (width, own_a)).astype(BF16)
+        c_down[k] = jnp.broadcast_to(0.5 * c_turned[:, k:k + 1], (width, own_a)).astype(BF16)
     sum_b[...] = jnp.zeros_like(sum_b)
     sum_c[...] = jnp.zeros_like(sum_c)
 
@@ -134,58 +135,104 @@
     if chips > 2:
         send_a(2).start()
     b_all = b_buf[...].reshape(n_samples * own_b, width)
-    b_turned[...] = (b_all.astype(F32) * 0.5).T.astype(BF16)
-
-    def step(t, carry):
-        pair = lax.div(t, 2)
-        even = lax.rem(t, 2) == 0
-        block = block_at(t)
-        arrived(a_buf.at[block], a_recv.at[block])
-
-        @pl.when(jnp.logical_and(even, t < n_space - 2))
+    b_wide = b_all.astype(F32) * 0.5
+    b_half[...] = b_wide.astype(BF16)
+    b_turned[...] = b_wide.T.astype(BF16)
+
+    def take(t):
+        arrived(a_buf.at[block_at(t)], a_recv.at[block_at(t)])
+
+        @pl.when(jnp.logical_and(lax.rem(t, 2) == 0, t < n_space - 2))
         def _():
             forward(t).start()
 
-        @pl.when(jnp.logical_and(even, pair + 3 < chips))
+        far = lax.div(t, 2) + 3
+
+        @pl.when(jnp.logical_and(lax.rem(t, 2) == 0, far < chips))
         def _():
-            send_far(pair + 3).start()
-
-        load(t).wait()
-        a = a_buf[block]
-        a_wide = a.astype(F32)
-        a_turned = a_wide.T.astype(BF16)
-        b_full = b_buf[...].reshape(n_samples * own_b, width)
-        total = jnp.zeros((own_a, width), F32)
-        for g, (d_buf, s_buf) in enumerate(((d_buf0, s_buf0), (d_buf1, s_buf1))):
+            send_far(far).start()
+
+    def stage_model(t, g):
+        a = a_buf[block_at(t)]
+        for j in range(GROUP):
+            x_buf[j * own_a:(j + 1) * own_a, :] = a * c_along[g * GROUP + j]
+        h_bufs[g][...] = matmul(x_buf[...], b_turned[...])
+
+    def stage_derivative(t, g):
+        for j in range(GROUP):
+            k = g * GROUP + j
+            s_bufs[g][:, j * own_a:(j + 1) * own_a] = a_turned[...] * c_down[k]
+            for r in range(0, own_a, CHUNK):
+                rows = slice(j * own_a + r, j * own_a + r + CHUNK)
+                entries = t_buf[t, k, r:r + CHUNK, :]
+                shift = 1.0 - (entries + entries).astype(F32)
+                d_bufs[g][rows, :] = (jnp.tanh(h_bufs[g][rows, :]) + shift).astype(BF16)
+
+    def stage_sums(t, g, a_rows):
+        inner_buf[...] = matmul(d_bufs[g][...], b_half[...])
+        over_c = [jnp.zeros((8, width), F32) for _ in range(GROUP)]
+        for r in range(0, own_a, CHUNK):
+            a_wide = a_rows(r)
+            total = part[t, r:r + CHUNK, :] if g else jnp.zeros((CHUNK, width), F32)
             for j in range(GROUP):
                 k = g * GROUP + j
-                rows = slice(j * own_a, (j + 1) * own_a)
-                half_model = matmul(a * c_along[k], b_turned[...])
-                derivative = (0.5 * jnp.tanh(half_model) + (0.5 - t_buf[t, k].astype(F32))).astype(BF16)
-                d_buf[rows, :] = derivative
-                s_buf[:, rows] = a_turned * c_down[k]
-                inner = matmul(derivative, b_full)
+                inner = inner_buf[j * own_a + r:j * own_a + r + CHUNK, :]
                 total = total + inner * c_ref[k:k + 1, :].astype(F32)
-                sum_c[k] += jnp.sum((a_wide * inner).reshape(own_a // 8, 8, width), axis=0)
-            sum_b[...] += matmul(s_buf[...], d_buf[...])
-        part[t] = total
-
-        last = t == n_space - 2
-
-        @pl.when(jnp.logical_or(last, jnp.logical_and(jnp.logical_not(even), t < n_space - 2)))
+                product = a_wide * inner
+                for q in range(0, CHUNK, 8):
+                    over_c[j] = over_c[j] + product[q:q + 8, :]
+            part[t, r:r + CHUNK, :] = total
+        for j in range(GROUP):
+            sum_c[g * GROUP + j] += over_c[j]
+        sum_b[...] += matmul(s_bufs[g][...], d_bufs[g][...])
+
+    def from_before(r):
+        return a_before[r:r + CHUNK, :]
+
+    def step(t, carry):
+        before = lax.rem(t + n_space - 1, n_space)
+        after = lax.rem(t + 1, n_space)
+        block = block_at(t)
+        load(t).wait()
+        a_turned[...] = a_buf[block].astype(F32).T.astype(BF16)
+        stage_model(t, 1)
+        stage_derivative(t, 0)
+        stage_sums(before, 1, from_before)
+
+        @pl.when(t > 0)
         def _():
-            to_sibling(t, pair).start()
-
-        @pl.when(jnp.logical_and(even, t >= 2))
+            pair = lax.div(before, 2)
+            even = lax.rem(before, 2) == 0
+            last = before == n_space - 2
+
+            @pl.when(jnp.logical_or(last, jnp.logical_and(jnp.logical_not(even), before < n_space - 2)))
+            def _():
+                to_sibling(before, pair).start()
+
+            @pl.when(jnp.logical_and(even, before >= 2))
+            def _():
+                ready = pair - 1
+                arrived(sib_part.at[ready], sib_recv.at[ready])
+                z_out[ready] = (part[before - 2] + sib_part[ready]).astype(BF16)
+                to_owner(ready).start()
+
+        @pl.when(t + 1 < n_space)
         def _():
-            before = pair - 1
-            arrived(sib_part.at[before], sib_recv.at[before])
-            z_out[before] = (part[t - 2] + sib_part[before]).astype(BF16)
-            to_owner(before).start()
-
+            take(after)
+
+        a_before[...] = a_buf[block].astype(F32)
+        stage_model(after, 0)
+        stage_derivative(t, 1)
+        stage_sums(t, 0, lambda r: a_buf[block, r:r + CHUNK, :].astype(F32))
         return carry
 
+    for buf in (d_bufs[1], s_bufs[1], a_before):
+        buf[...] = jnp.zeros_like(buf)
+    part[n_space - 1] = jnp.zeros((own_a, width), F32)
+    take(jnp.int32(0))
+    stage_model(jnp.int32(0), 0)
     lax.fori_loop(0, n_space, step, 0)
+    stage_sums(n_space - 1, 1, from_before)
 
     for k in range(steps):
         c_in[m, pl.ds(k, 1), :] = jnp.sum(sum_c[k], axis=0, keepdims=True)
@@ -237,6 +284,15 @@
         send_gd(i).wait_send()
 
 
+def hand_over(in_a, in_b, in_c, out_a, out_b, out_c, sem):
+    pairs = ((in_a, out_a), (in_b, out_b), (in_c, out_c))
+    copies = [pltpu.make_async_copy(x, y, sem.at[i]) for i, (x, y) in enumerate(pairs)]
+    for copy in copies:
+        copy.start()
+    for copy in copies:
+        copy.wait()
+
+
 def on_device(n_samples, n_space, target, a_factor, b_factor, c_factor):
     steps, rows, columns = target.shape
     own_a, width = a_factor.shape
@@ -246,7 +302,7 @@
     flops = 6 * steps * rows * columns * width
     anywhere = pl.BlockSpec(memory_space=pl.ANY)
     inside = pl.BlockSpec(memory_space=pltpu.VMEM)
-    return pl.pallas_call(
+    grads = pl.pallas_call(
         functools.partial(kernel, n_samples, n_space),
         out_shape=(
             jax.ShapeDtypeStruct((own_a, width), F32),
@@ -259,13 +315,17 @@
             vmem((n_space, steps, own_a, columns), BF16),
             vmem((n_space, own_a, width), BF16),
             vmem((n_samples, own_b, width), BF16),
+            vmem((columns, width), BF16),
             vmem((width, columns), BF16),
             vmem((steps, width, own_a), BF16),
             vmem((steps, own_a, width), BF16),
-            vmem((GROUP * own_a, columns), BF16),
-            vmem((GROUP * own_a, columns), BF16),
-            vmem((width, GROUP * own_a), BF16),
-            vmem((width, GROUP * own_a), BF16),
+            [vmem((GROUP * own_a, columns), F32)] * 2,
+            [vmem((GROUP * own_a, columns), BF16)] * 2,
+            [vmem((width, GROUP * own_a), BF16)] * 2,
+            vmem((GROUP * own_a, width), BF16),
+            vmem((GROUP * own_a, width), F32),
+            vmem((width, own_a), BF16),
+            vmem((own_a, width), F32),
             vmem((width, columns), F32),
             vmem((steps, 8, width), F32),
             vmem((n_space, own_a, width), F32),
@@ -291,6 +351,15 @@
         ),
         name="cp_gradient",
     )(target, a_factor, b_factor, c_factor)
+    return pl.pallas_call(
+        hand_over,
+        out_shape=tuple(jax.ShapeDtypeStruct(g.shape, g.dtype) for g in grads),
+        in_specs=[anywhere] * 3,
+        out_specs=(anywhere,) * 3,
+        scratch_shapes=[dma((3,))],
+        compiler_params=pltpu.CompilerParams(vmem_limit_bytes=56 * 1024 * 1024),
+        name="hand_over",
+    )(*grads)
 
 
 def solution(mesh):

time: 48.7 us -> 63.1 us (1.30)
  Pallas kernels: 43.2 us -> 62.3 us
  local copies, waits for them, and re-layouts: 4.53 us -> 0 us
    pallas_call x0 -> x1, Pallas kernels: none -> 13.3 us  [on_device(): pl.pallas_call(hand_over, out_shape=tuple((jax.ShapeDtypeStruct(g.shape,...]
    pallas_call x1, Pallas kernels: 43.2 us -> 49 us  [on_device(): pl.pallas_call(functools.partial(kernel, n_samples, n_space), out_shape=(...]
    unnamed x3 -> x0, local copies, waits for them, and re-layouts: 4.53 us -> none
where the time goes in v2:
time: 63.1 us; the launch traced here: 62.9 us
  Pallas kernels  62.3 us (99%)
  between operations  0.64 us (1%)
    pallas_call x1, Pallas kernels, on_device(): pl.pallas_call(functools.partial(kernel, n_samples, n_space), out_shape=(...  49 us
    pallas_call x1, Pallas kernels, on_device(): pl.pallas_call(hand_over, out_shape=tuple((jax.ShapeDtypeStruct(g.shape,...  13.3 us

profile of v2, /device:TPU:0, one launch (start us, length us, event | category | flops | bytes accessed | tf_op | source)
XLA Modules:
  0.0 62.9 jit_solution(16508535455891523493)
XLA Ops:
  0.6 49.0 %cp_gradient.1 = (f32[256,256]{1,0:T(8,128)}, f32[128,256]{1,0:T(8,128)}, f32[8,256]{1,0:T(8,128)}) custom-call(bf16[8,2048,512]{2,1,0:T(8,128)(2,1)} %target.1, bf16[256,256]{1,0:T(8,128)(2,1)} %a_own.1, bf16[128,256]{1,0:T(8,128)(2,1)} %b_own.1, bf16[8,256]{1,0:T(8,128)(2,1)} %c_ref.1), custom_call_target="tpu_custom_call" | custom-call | flops 12884901888 | bytes 16777216 | tf_op jit(solution)/shard_map/cp_gradient/pallas_call | solution.py:305
  49.6 13.3 %hand_over.1 = (f32[256,256]{1,0:T(8,128)}, f32[128,256]{1,0:T(8,128)}, f32[8,256]{1,0:T(8,128)}) custom-call(f32[256,256]{1,0:T(8,128)} %get-tuple-element.6.in_a, f32[128,256]{1,0:T(8,128)} %get-tuple-element.7.in_b, f32[8,256]{1,0:T(8,128)} %get-tuple-element.8.in_c), custom_call_target="tpu_custom_call" | custom-call | tf_op jit(solution)/shard_map/hand_over/pallas_call | solution.py:354

commit v3 on v1

--- a/solution.py
+++ b/solution.py
@@ -10,7 +10,7 @@
 MESH = pl.DeviceIdType.MESH
 F32 = jnp.float32
 BF16 = jnp.bfloat16
-GROUP = 4
+CHUNK = 32
 
 
 def matmul(x, y):
@@ -21,8 +21,8 @@
     n_samples, n_space,
     target, a_own, b_own, c_ref,
     grad_a, grad_b, grad_c,
-    t_buf, a_buf, b_buf, b_turned, c_down, c_along,
-    d_buf0, d_buf1, s_buf0, s_buf1,
+    t_buf, a_buf, b_buf, b_half, b_turned, c_down, c_along,
+    d_bufs, s_bufs,
     sum_b, sum_c, part, sib_part, z_out, z_in, b_out, b_in, c_in, c_all,
     t_sem, a_recv, b_recv, b_send, a_send, fwd_send,
     sib_send, sib_recv, z_send, z_recv, gb_send, gb_recv,
@@ -122,7 +122,7 @@
     c_turned = c_wide.T
     for k in range(steps):
         c_along[k] = jnp.broadcast_to(c_wide[k:k + 1, :], (own_a, width)).astype(BF16)
-        c_down[k] = jnp.broadcast_to(c_turned[:, k:k + 1], (width, own_a)).astype(BF16)
+        c_down[k] = jnp.broadcast_to(0.5 * c_turned[:, k:k + 1], (width, own_a)).astype(BF16)
     sum_b[...] = jnp.zeros_like(sum_b)
     sum_c[...] = jnp.zeros_like(sum_c)
 
@@ -134,41 +134,65 @@
     if chips > 2:
         send_a(2).start()
     b_all = b_buf[...].reshape(n_samples * own_b, width)
-    b_turned[...] = (b_all.astype(F32) * 0.5).T.astype(BF16)
+    b_wide = b_all.astype(F32) * 0.5
+    b_half[...] = b_wide.astype(BF16)
+    b_turned[...] = b_wide.T.astype(BF16)
+
+    def take(t):
+        arrived(a_buf.at[block_at(t)], a_recv.at[block_at(t)])
+
+        @pl.when(jnp.logical_and(lax.rem(t, 2) == 0, t < n_space - 2))
+        def _():
+            forward(t).start()
+
+        far = lax.div(t, 2) + 3
+
+        @pl.when(jnp.logical_and(lax.rem(t, 2) == 0, far < chips))
+        def _():
+            send_far(far).start()
 
     def step(t, carry):
         pair = lax.div(t, 2)
         even = lax.rem(t, 2) == 0
         block = block_at(t)
-        arrived(a_buf.at[block], a_recv.at[block])
-
-        @pl.when(jnp.logical_and(even, t < n_space - 2))
-        def _():
-            forward(t).start()
-
-        @pl.when(jnp.logical_and(even, pair + 3 < chips))
-        def _():
-            send_far(pair + 3).start()
-
+        take(t)
         load(t).wait()
         a = a_buf[block]
         a_wide = a.astype(F32)
         a_turned = a_wide.T.astype(BF16)
-        b_full = b_buf[...].reshape(n_samples * own_b, width)
+
+        def model(k):
+            return matmul(a * c_along[k], b_turned[...])
+
+        def slot(k):
+            return k // 2 % 2, slice(k % 2 * own_a, (k % 2 + 1) * own_a)
+
+        def derive(k, half_model):
+            g, rows = slot(k)
+            for r in range(0, own_a, CHUNK):
+                entries = t_buf[t, k, r:r + CHUNK, :]
+                shift = 1.0 - (entries + entries).astype(F32)
+                found = (jnp.tanh(half_model[r:r + CHUNK]) + shift).astype(BF16)
+                d_bufs[g][rows.start + r:rows.start + r + CHUNK, :] = found
+            s_bufs[g][:, rows] = a_turned * c_down[k]
+
+        def add_up(k, total):
+            g, rows = slot(k)
+            inner = matmul(d_bufs[g][rows, :], b_half[...])
+            sum_c[k] += jnp.sum((a_wide * inner).reshape(own_a // 8, 8, width), axis=0)
+            if k % 2:
+                sum_b[...] += matmul(s_bufs[g][...], d_bufs[g][...])
+            return total + inner * c_ref[k:k + 1, :].astype(F32)
+
         total = jnp.zeros((own_a, width), F32)
-        for g, (d_buf, s_buf) in enumerate(((d_buf0, s_buf0), (d_buf1, s_buf1))):
-            for j in range(GROUP):
-                k = g * GROUP + j
-                rows = slice(j * own_a, (j + 1) * own_a)
-                half_model = matmul(a * c_along[k], b_turned[...])
-                derivative = (0.5 * jnp.tanh(half_model) + (0.5 - t_buf[t, k].astype(F32))).astype(BF16)
-                d_buf[rows, :] = derivative
-                s_buf[:, rows] = a_turned * c_down[k]
-                inner = matmul(derivative, b_full)
-                total = total + inner * c_ref[k:k + 1, :].astype(F32)
-                sum_c[k] += jnp.sum((a_wide * inner).reshape(own_a // 8, 8, width), axis=0)
-            sum_b[...] += matmul(s_buf[...], d_buf[...])
-        part[t] = total
+        now = model(0)
+        for k in range(steps):
+            later = model(k + 1) if k + 1 < steps else None
+            derive(k, now)
+            if k:
+                total = add_up(k - 1, total)
+            now = later
+        part[t] = add_up(steps - 1, total)
 
         last = t == n_space - 2
 
@@ -237,6 +261,18 @@
         send_gd(i).wait_send()
 
 
+def hand_over(in_a, in_b, in_c, out_a, out_b, out_c, via_a, via_b, via_c, sem):
+    def copies(sources, targets):
+        started = [pltpu.make_async_copy(x, y, sem.at[i]) for i, (x, y) in enumerate(zip(sources, targets))]
+        for copy in started:
+            copy.start()
+        for copy in started:
+            copy.wait()
+
+    copies((in_a, in_b, in_c), (via_a, via_b, via_c))
+    copies((via_a, via_b, via_c), (out_a, out_b, out_c))
+
+
 def on_device(n_samples, n_space, target, a_factor, b_factor, c_factor):
     steps, rows, columns = target.shape
     own_a, width = a_factor.shape
@@ -246,7 +282,7 @@
     flops = 6 * steps * rows * columns * width
     anywhere = pl.BlockSpec(memory_space=pl.ANY)
     inside = pl.BlockSpec(memory_space=pltpu.VMEM)
-    return pl.pallas_call(
+    grads = pl.pallas_call(
         functools.partial(kernel, n_samples, n_space),
         out_shape=(
             jax.ShapeDtypeStruct((own_a, width), F32),
@@ -259,13 +295,12 @@
             vmem((n_space, steps, own_a, columns), BF16),
             vmem((n_space, own_a, width), BF16),
             vmem((n_samples, own_b, width), BF16),
+            vmem((columns, width), BF16),
             vmem((width, columns), BF16),
             vmem((steps, width, own_a), BF16),
             vmem((steps, own_a, width), BF16),
-            vmem((GROUP * own_a, columns), BF16),
-            vmem((GROUP * own_a, columns), BF16),
-            vmem((width, GROUP * own_a), BF16),
-            vmem((width, GROUP * own_a), BF16),
+            [vmem((2 * own_a, columns), BF16)] * 2,
+            [vmem((width, 2 * own_a), BF16)] * 2,
             vmem((width, columns), F32),
             vmem((steps, 8, width), F32),
             vmem((n_space, own_a, width), F32),
@@ -291,6 +326,15 @@
         ),
         name="cp_gradient",
     )(target, a_factor, b_factor, c_factor)
+    return pl.pallas_call(
+        hand_over,
+        out_shape=tuple(jax.ShapeDtypeStruct(g.shape, g.dtype) for g in grads),
+        in_specs=[anywhere] * 3,
+        out_specs=(anywhere,) * 3,
+        scratch_shapes=[vmem(g.shape, g.dtype) for g in grads] + [dma((3,))],
+        compiler_params=pltpu.CompilerParams(vmem_limit_bytes=56 * 1024 * 1024),
+        name="hand_over",
+    )(*grads)
 
 
 def solution(mesh):

time: 48.7 us -> 45.5 us (0.934)
  local copies, waits for them, and re-layouts: 4.53 us -> 0 us
  Pallas kernels: 43.2 us -> 44.6 us
    unnamed x3 -> x0, local copies, waits for them, and re-layouts: 4.53 us -> none
    pallas_call x0 -> x1, Pallas kernels: none -> 1.75 us  [on_device(): pl.pallas_call(hand_over, out_shape=tuple((jax.ShapeDtypeStruct(g.shape,...]
where the time goes in v3:
time: 45.5 us; the launch traced here: 45.3 us
  Pallas kernels  44.6 us (98%)
  between operations  0.64 us (1%)
    pallas_call x1, Pallas kernels, on_device(): pl.pallas_call(functools.partial(kernel, n_samples, n_space), out_shape=(...  42.9 us
    pallas_call x1, Pallas kernels, on_device(): pl.pallas_call(hand_over, out_shape=tuple((jax.ShapeDtypeStruct(g.shape,...  1.75 us

profile of v3, /device:TPU:0, one launch (start us, length us, event | category | flops | bytes accessed | tf_op | source)
XLA Modules:
  0.0 45.3 jit_solution(12683895344319939155)
XLA Ops:
  0.6 42.9 %cp_gradient.1 = (f32[256,256]{1,0:T(8,128)}, f32[128,256]{1,0:T(8,128)}, f32[8,256]{1,0:T(8,128)}) custom-call(bf16[8,2048,512]{2,1,0:T(8,128)(2,1)} %target.1, bf16[256,256]{1,0:T(8,128)(2,1)} %a_own.1, bf16[128,256]{1,0:T(8,128)(2,1)} %b_own.1, bf16[8,256]{1,0:T(8,128)(2,1)} %c_ref.1), custom_call_target="tpu_custom_call" | custom-call | flops 12884901888 | bytes 16777216 | tf_op jit(solution)/shard_map/cp_gradient/pallas_call | solution.py:285
  43.5 1.8 %hand_over.1 = (f32[256,256]{1,0:T(8,128)}, f32[128,256]{1,0:T(8,128)}, f32[8,256]{1,0:T(8,128)}) custom-call(f32[256,256]{1,0:T(8,128)} %get-tuple-element.6.in_a, f32[128,256]{1,0:T(8,128)} %get-tuple-element.7.in_b, f32[8,256]{1,0:T(8,128)} %get-tuple-element.8.in_c), custom_call_target="tpu_custom_call" | custom-call | tf_op jit(solution)/shard_map/hand_over/pallas_call | solution.py:329

commit v4 on v3

--- a/solution.py
+++ b/solution.py
@@ -45,9 +45,9 @@
         return found
 
     def block_at(t):
-        pair, half = lax.div(t, 2), lax.rem(t, 2)
-        flip = lax.div(pair + 1, chips)
-        return other(lax.rem(pair + 1, chips)) * 2 + lax.rem(core + half + flip, 2)
+        d, half = lax.rem(lax.div(t + 1, 2), chips), lax.rem(t + 1, 2)
+        flip = lax.div(chips - d, chips)
+        return other(d) * 2 + lax.rem(core + half + flip, 2)
 
     def load(t):
         rows = pl.ds(pl.multiple_of(block_at(t) * own_a, own_a), own_a)
@@ -68,9 +68,6 @@
     def send_a(d):
         to = sibling if d == 0 else other(d) * 2 + core
         return send(a_own, a_buf.at[s], a_send.at[d], a_recv.at[s], space=to)
-
-    def send_far(d):
-        return send(a_own, a_buf.at[s], a_send.at[d], a_recv.at[s], space=other(d) * 2 + core)
 
     def forward(t):
         block = a_buf.at[block_at(t)]
@@ -109,7 +106,8 @@
 
     for i in range(1, n_samples):
         send_b(i).start()
-    send_a(1).start()
+    for d in range(1, chips):
+        send_a(d).start()
     send_a(0).start()
 
     def start_load(t, carry):
@@ -131,8 +129,6 @@
         return carry
 
     lax.fori_loop(0, n_samples, wait_b, 0)
-    if chips > 2:
-        send_a(2).start()
     b_all = b_buf[...].reshape(n_samples * own_b, width)
     b_wide = b_all.astype(F32) * 0.5
     b_half[...] = b_wide.astype(BF16)
@@ -141,19 +137,20 @@
     def take(t):
         arrived(a_buf.at[block_at(t)], a_recv.at[block_at(t)])
 
-        @pl.when(jnp.logical_and(lax.rem(t, 2) == 0, t < n_space - 2))
+        @pl.when(jnp.logical_and(lax.rem(t, 2) == 1, t < n_space - 1))
         def _():
             forward(t).start()
 
-        far = lax.div(t, 2) + 3
-
-        @pl.when(jnp.logical_and(lax.rem(t, 2) == 0, far < chips))
+    def combine(t, odd):
+        @pl.when(jnp.logical_and(odd, t >= 3))
         def _():
-            send_far(far).start()
+            ready = lax.div(t, 2) - 1
+            arrived(sib_part.at[ready], sib_recv.at[ready])
+            z_out[ready] = (part[t - 2] + sib_part[ready]).astype(BF16)
+            to_owner(ready).start()
 
     def step(t, carry):
-        pair = lax.div(t, 2)
-        even = lax.rem(t, 2) == 0
+        odd = lax.rem(t, 2) == 1
         block = block_at(t)
         take(t)
         load(t).wait()
@@ -192,20 +189,13 @@
             if k:
                 total = add_up(k - 1, total)
             now = later
+            if k == steps // 2:
+                combine(t, odd)
         part[t] = add_up(steps - 1, total)
 
-        last = t == n_space - 2
-
-        @pl.when(jnp.logical_or(last, jnp.logical_and(jnp.logical_not(even), t < n_space - 2)))
+        @pl.when(jnp.logical_or(t == n_space - 1, jnp.logical_and(jnp.logical_not(odd), t > 0)))
         def _():
-            to_sibling(t, pair).start()
-
-        @pl.when(jnp.logical_and(even, t >= 2))
-        def _():
-            before = pair - 1
-            arrived(sib_part.at[before], sib_recv.at[before])
-            z_out[before] = (part[t - 2] + sib_part[before]).astype(BF16)
-            to_owner(before).start()
+            to_sibling(t, lax.div(t + 1, 2) - 1).start()
 
         return carry
 
@@ -221,7 +211,7 @@
         send_gb(i).start()
 
     arrived(sib_part.at[chips - 1], sib_recv.at[chips - 1])
-    total = part[n_space - 1] + sib_part[chips - 1]
+    total = part[0] + sib_part[chips - 1]
     for pair in range(chips - 1):
         arrived(z_in.at[pair], z_recv.at[pair])
         total = total + z_in[pair].astype(F32)
@@ -253,10 +243,10 @@
     for d in range(chips):
         send_a(d).wait_send()
     for pair in range(chips - 1):
-        forward(jnp.int32(2 * pair)).wait_send()
+        forward(jnp.int32(2 * pair + 1)).wait_send()
         to_owner(pair).wait_send()
-        to_sibling(2 * pair + 1, pair).wait_send()
-    to_sibling(n_space - 2, chips - 1).wait_send()
+        to_sibling(2 * pair + 2, pair).wait_send()
+    to_sibling(n_space - 1, chips - 1).wait_send()
     for i in range(1, n_space):
         send_gd(i).wait_send()
 

time: 45.5 us -> 43.3 us (0.952)
  Pallas kernels: 44.6 us -> 42.5 us
    pallas_call x1, Pallas kernels: 42.9 us -> 40.8 us  [on_device(): pl.pallas_call(functools.partial(kernel, n_samples, n_space), out_shape=(...]
where the time goes in v4:
time: 43.3 us; the launch traced here: 43.2 us
  Pallas kernels  42.5 us (98%)
  between operations  0.64 us (1%)
    pallas_call x1, Pallas kernels, on_device(): pl.pallas_call(functools.partial(kernel, n_samples, n_space), out_shape=(...  40.8 us
    pallas_call x1, Pallas kernels, on_device(): pl.pallas_call(hand_over, out_shape=tuple((jax.ShapeDtypeStruct(g.shape,...  1.75 us

profile of v4, /device:TPU:0, one launch (start us, length us, event | category | flops | bytes accessed | tf_op | source)
XLA Modules:
  0.0 43.2 jit_solution(15537430558414492339)
XLA Ops:
  0.6 40.8 %cp_gradient.1 = (f32[256,256]{1,0:T(8,128)}, f32[128,256]{1,0:T(8,128)}, f32[8,256]{1,0:T(8,128)}) custom-call(bf16[8,2048,512]{2,1,0:T(8,128)(2,1)} %target.1, bf16[256,256]{1,0:T(8,128)(2,1)} %a_own.1, bf16[128,256]{1,0:T(8,128)(2,1)} %b_own.1, bf16[8,256]{1,0:T(8,128)(2,1)} %c_ref.1), custom_call_target="tpu_custom_call" | custom-call | flops 12884901888 | bytes 16777216 | tf_op jit(solution)/shard_map/cp_gradient/pallas_call | solution.py:275
  41.4 1.8 %hand_over.1 = (f32[256,256]{1,0:T(8,128)}, f32[128,256]{1,0:T(8,128)}, f32[8,256]{1,0:T(8,128)}) custom-call(f32[256,256]{1,0:T(8,128)} %get-tuple-element.6.in_a, f32[128,256]{1,0:T(8,128)} %get-tuple-element.7.in_b, f32[8,256]{1,0:T(8,128)} %get-tuple-element.8.in_c), custom_call_target="tpu_custom_call" | custom-call | tf_op jit(solution)/shard_map/hand_over/pallas_call | solution.py:319

commit v5 on v4

--- a/solution.py
+++ b/solution.py
@@ -10,6 +10,7 @@
 MESH = pl.DeviceIdType.MESH
 F32 = jnp.float32
 BF16 = jnp.bfloat16
+GROUP = 4
 CHUNK = 32
 
 
@@ -44,10 +45,13 @@
             bit *= 2
         return found
 
+    def distance(turn):
+        return lax.rem(turn, chips - 1) + lax.div(turn + chips - 1, chips) if chips > 1 else turn
+
     def block_at(t):
-        d, half = lax.rem(lax.div(t + 1, 2), chips), lax.rem(t + 1, 2)
-        flip = lax.div(chips - d, chips)
-        return other(d) * 2 + lax.rem(core + half + flip, 2)
+        turn, half = lax.rem(lax.div(t + 1, 2), chips), lax.rem(t + 1, 2)
+        flip = lax.div(chips - turn, chips)
+        return other(distance(turn)) * 2 + lax.rem(core + half + flip, 2)
 
     def load(t):
         rows = pl.ds(pl.multiple_of(block_at(t) * own_a, own_a), own_a)
@@ -79,7 +83,7 @@
     def to_owner(pair):
         return send(
             z_out.at[pair], z_in.at[pair], z_send.at[pair], z_recv.at[pair],
-            space=other(pair + 1) * 2 + core,
+            space=other(distance(jnp.int32(pair + 1))) * 2 + core,
         )
 
     def send_gb(i):
@@ -106,8 +110,8 @@
 
     for i in range(1, n_samples):
         send_b(i).start()
-    for d in range(1, chips):
-        send_a(d).start()
+    for turn in range(1, chips):
+        send_a(turn % (chips - 1) + 1).start()
     send_a(0).start()
 
     def start_load(t, carry):
@@ -155,43 +159,45 @@
         take(t)
         load(t).wait()
         a = a_buf[block]
-        a_wide = a.astype(F32)
-        a_turned = a_wide.T.astype(BF16)
-
-        def model(k):
-            return matmul(a * c_along[k], b_turned[...])
-
-        def slot(k):
-            return k // 2 % 2, slice(k % 2 * own_a, (k % 2 + 1) * own_a)
-
-        def derive(k, half_model):
-            g, rows = slot(k)
+        a_turned = a.astype(F32).T.astype(BF16)
+
+        def derive(k):
+            g, j = k // GROUP, k % GROUP
+            half_model = matmul(a * c_along[k], b_turned[...])
             for r in range(0, own_a, CHUNK):
                 entries = t_buf[t, k, r:r + CHUNK, :]
                 shift = 1.0 - (entries + entries).astype(F32)
                 found = (jnp.tanh(half_model[r:r + CHUNK]) + shift).astype(BF16)
-                d_bufs[g][rows.start + r:rows.start + r + CHUNK, :] = found
-            s_bufs[g][:, rows] = a_turned * c_down[k]
-
-        def add_up(k, total):
-            g, rows = slot(k)
-            inner = matmul(d_bufs[g][rows, :], b_half[...])
-            sum_c[k] += jnp.sum((a_wide * inner).reshape(own_a // 8, 8, width), axis=0)
-            if k % 2:
-                sum_b[...] += matmul(s_bufs[g][...], d_bufs[g][...])
-            return total + inner * c_ref[k:k + 1, :].astype(F32)
-
-        total = jnp.zeros((own_a, width), F32)
-        now = model(0)
-        for k in range(steps):
-            later = model(k + 1) if k + 1 < steps else None
-            derive(k, now)
-            if k:
-                total = add_up(k - 1, total)
-            now = later
-            if k == steps // 2:
+                d_bufs[g][j * own_a + r:j * own_a + r + CHUNK, :] = found
+            s_bufs[g][:, j * own_a:(j + 1) * own_a] = a_turned * c_down[k]
+
+        def add_inner(k):
+            g, j = k // GROUP, k % GROUP
+            inner = matmul(d_bufs[g][j * own_a:(j + 2) * own_a, :], b_half[...])
+            over_c = [jnp.zeros((8, width), F32)] * 2
+            for r in range(0, own_a, CHUNK):
+                a_rows = a_buf[block, r:r + CHUNK, :].astype(F32)
+                total = part[t, r:r + CHUNK, :] if k else jnp.zeros((CHUNK, width), F32)
+                for i in range(2):
+                    piece = inner[i * own_a + r:i * own_a + r + CHUNK]
+                    total = total + piece * c_ref[k + i:k + i + 1, :].astype(F32)
+                    over_c[i] = over_c[i] + jnp.sum((a_rows * piece).reshape(CHUNK // 8, 8, width), axis=0)
+                part[t, r:r + CHUNK, :] = total
+            for i in range(2):
+                sum_c[k + i] += over_c[i]
+
+        def add_b(g):
+            sum_b[...] += matmul(s_bufs[g][...], d_bufs[g][...])
+
+        for k in range(0, steps, 2):
+            if k == GROUP:
                 combine(t, odd)
-        part[t] = add_up(steps - 1, total)
+            derive(k)
+            derive(k + 1)
+            if k and k % GROUP == 0:
+                add_b(k // GROUP - 1)
+            add_inner(k)
+        add_b(steps // GROUP - 1)
 
         @pl.when(jnp.logical_or(t == n_space - 1, jnp.logical_and(jnp.logical_not(odd), t > 0)))
         def _():
@@ -289,8 +295,8 @@
             vmem((width, columns), BF16),
             vmem((steps, width, own_a), BF16),
             vmem((steps, own_a, width), BF16),
-            [vmem((2 * own_a, columns), BF16)] * 2,
-            [vmem((width, 2 * own_a), BF16)] * 2,
+            [vmem((GROUP * own_a, columns), BF16)] * (steps // GROUP),
+            [vmem((width, GROUP * own_a), BF16)] * (steps // GROUP),
             vmem((width, columns), F32),
             vmem((steps, 8, width), F32),
             vmem((n_space, own_a, width), F32),

time: 43.3 us -> 46.4 us (1.072)
  Pallas kernels: 42.5 us -> 45.6 us
    pallas_call x1, Pallas kernels: 40.8 us -> 43.9 us  [on_device(): pl.pallas_call(functools.partial(kernel, n_samples, n_space), out_shape=(...]
where the time goes in v5:
time: 46.4 us; the launch traced here: 46.3 us
  Pallas kernels  45.6 us (98%)
  between operations  0.64 us (1%)
    pallas_call x1, Pallas kernels, on_device(): pl.pallas_call(functools.partial(kernel, n_samples, n_space), out_shape=(...  43.9 us
    pallas_call x1, Pallas kernels, on_device(): pl.pallas_call(hand_over, out_shape=tuple((jax.ShapeDtypeStruct(g.shape,...  1.75 us

profile of v5, /device:TPU:0, one launch (start us, length us, event | category | flops | bytes accessed | tf_op | source)
XLA Modules:
  0.0 46.3 jit_solution(14243746934319325499)
XLA Ops:
  0.6 43.9 %cp_gradient.1 = (f32[256,256]{1,0:T(8,128)}, f32[128,256]{1,0:T(8,128)}, f32[8,256]{1,0:T(8,128)}) custom-call(bf16[8,2048,512]{2,1,0:T(8,128)(2,1)} %target.1, bf16[256,256]{1,0:T(8,128)(2,1)} %a_own.1, bf16[128,256]{1,0:T(8,128)(2,1)} %b_own.1, bf16[8,256]{1,0:T(8,128)(2,1)} %c_ref.1), custom_call_target="tpu_custom_call" | custom-call | flops 12884901888 | bytes 16777216 | tf_op jit(solution)/shard_map/cp_gradient/pallas_call | solution.py:281
  44.5 1.8 %hand_over.1 = (f32[256,256]{1,0:T(8,128)}, f32[128,256]{1,0:T(8,128)}, f32[8,256]{1,0:T(8,128)}) custom-call(f32[256,256]{1,0:T(8,128)} %get-tuple-element.6.in_a, f32[128,256]{1,0:T(8,128)} %get-tuple-element.7.in_b, f32[8,256]{1,0:T(8,128)} %get-tuple-element.8.in_c), custom_call_target="tpu_custom_call" | custom-call | tf_op jit(solution)/shard_map/hand_over/pallas_call | solution.py:325

commit v6 on v4

--- a/solution.py
+++ b/solution.py
@@ -149,7 +149,10 @@
             z_out[ready] = (part[t - 2] + sib_part[ready]).astype(BF16)
             to_owner(ready).start()
 
-    def step(t, carry):
+    columns = b_turned.shape[1]
+    halves = (slice(0, columns // 2), slice(columns // 2, columns))
+
+    def step(t, carry, peeled=False):
         odd = lax.rem(t, 2) == 1
         block = block_at(t)
         take(t)
@@ -158,48 +161,61 @@
         a_wide = a.astype(F32)
         a_turned = a_wide.T.astype(BF16)
 
-        def model(k):
-            return matmul(a * c_along[k], b_turned[...])
+        def model(k, part_of):
+            return matmul(a * c_along[k], b_turned[:, part_of])
 
         def slot(k):
             return k // 2 % 2, slice(k % 2 * own_a, (k % 2 + 1) * own_a)
 
-        def derive(k, half_model):
+        def derive(k, half_model, part_of):
             g, rows = slot(k)
             for r in range(0, own_a, CHUNK):
-                entries = t_buf[t, k, r:r + CHUNK, :]
+                entries = t_buf[t, k, r:r + CHUNK, part_of]
                 shift = 1.0 - (entries + entries).astype(F32)
                 found = (jnp.tanh(half_model[r:r + CHUNK]) + shift).astype(BF16)
-                d_bufs[g][rows.start + r:rows.start + r + CHUNK, :] = found
-            s_bufs[g][:, rows] = a_turned * c_down[k]
-
-        def add_up(k, total):
+                d_bufs[g][rows.start + r:rows.start + r + CHUNK, part_of] = found
+
+        def add_inner(k, total):
             g, rows = slot(k)
-            inner = matmul(d_bufs[g][rows, :], b_half[...])
+            inner = sum(matmul(d_bufs[g][rows, part_of], b_half[part_of, :]) for part_of in halves)
             sum_c[k] += jnp.sum((a_wide * inner).reshape(own_a // 8, 8, width), axis=0)
-            if k % 2:
-                sum_b[...] += matmul(s_bufs[g][...], d_bufs[g][...])
             return total + inner * c_ref[k:k + 1, :].astype(F32)
 
+        def add_b(k, part_of):
+            g, _ = slot(k)
+            sum_b[:, part_of] += matmul(s_bufs[g][...], d_bufs[g][:, part_of])
+
         total = jnp.zeros((own_a, width), F32)
-        now = model(0)
-        for k in range(steps):
-            later = model(k + 1) if k + 1 < steps else None
-            derive(k, now)
+        now = [model(0, part_of) for part_of in halves]
+        for k in range(steps + 1):
+            later = []
+            for part_of, found in zip(halves, now if now else (None, None)):
+                if k + 1 < steps:
+                    later.append(model(k + 1, part_of))
+                if k < steps:
+                    derive(k, found, part_of)
+                if k and k % 2 == 0:
+                    add_b(k - 1, part_of)
+            if k < steps:
+                g, rows = slot(k)
+                s_bufs[g][:, rows] = a_turned * c_down[k]
             if k:
-                total = add_up(k - 1, total)
+                total = add_inner(k - 1, total)
             now = later
-            if k == steps // 2:
+            if peeled and k == steps // 2:
                 combine(t, odd)
-        part[t] = add_up(steps - 1, total)
+        part[t] = total
 
         @pl.when(jnp.logical_or(t == n_space - 1, jnp.logical_and(jnp.logical_not(odd), t > 0)))
         def _():
             to_sibling(t, lax.div(t + 1, 2) - 1).start()
 
+        if not peeled:
+            combine(t, odd)
         return carry
 
-    lax.fori_loop(0, n_space, step, 0)
+    lax.fori_loop(0, n_space - 1, step, 0)
+    step(jnp.int32(n_space - 1), 0, peeled=True)
 
     for k in range(steps):
         c_in[m, pl.ds(k, 1), :] = jnp.sum(sum_c[k], axis=0, keepdims=True)

time: 43.3 us -> 43.5 us (level)
  no operation moved by 1% of the time
where the time goes in v6:
time: 43.5 us; the launch traced here: 43.3 us
  Pallas kernels  42.6 us (98%)
  between operations  0.64 us (1%)
    pallas_call x1, Pallas kernels, on_device(): pl.pallas_call(functools.partial(kernel, n_samples, n_space), out_shape=(...  40.9 us
    pallas_call x1, Pallas kernels, on_device(): pl.pallas_call(hand_over, out_shape=tuple((jax.ShapeDtypeStruct(g.shape,...  1.75 us

profile of v6, /device:TPU:0, one launch (start us, length us, event | category | flops | bytes accessed | tf_op | source)
XLA Modules:
  0.0 43.3 jit_solution(1091228569615283758)
XLA Ops:
  0.6 40.9 %cp_gradient.1 = (f32[256,256]{1,0:T(8,128)}, f32[128,256]{1,0:T(8,128)}, f32[8,256]{1,0:T(8,128)}) custom-call(bf16[8,2048,512]{2,1,0:T(8,128)(2,1)} %target.1, bf16[256,256]{1,0:T(8,128)(2,1)} %a_own.1, bf16[128,256]{1,0:T(8,128)(2,1)} %b_own.1, bf16[8,256]{1,0:T(8,128)(2,1)} %c_ref.1), custom_call_target="tpu_custom_call" | custom-call | flops 12884901888 | bytes 16777216 | tf_op jit(solution)/shard_map/cp_gradient/pallas_call | solution.py:291
  41.5 1.8 %hand_over.1 = (f32[256,256]{1,0:T(8,128)}, f32[128,256]{1,0:T(8,128)}, f32[8,256]{1,0:T(8,128)}) custom-call(f32[256,256]{1,0:T(8,128)} %get-tuple-element.6.in_a, f32[128,256]{1,0:T(8,128)} %get-tuple-element.7.in_b, f32[8,256]{1,0:T(8,128)} %get-tuple-element.8.in_c), custom_call_target="tpu_custom_call" | custom-call | tf_op jit(solution)/shard_map/hand_over/pallas_call | solution.py:335

commit v7 on v4

--- a/solution.py
+++ b/solution.py
@@ -69,6 +69,9 @@
         to = sibling if d == 0 else other(d) * 2 + core
         return send(a_own, a_buf.at[s], a_send.at[d], a_recv.at[s], space=to)
 
+    def send_far(d):
+        return send(a_own, a_buf.at[s], a_send.at[d], a_recv.at[s], space=other(d) * 2 + core)
+
     def forward(t):
         block = a_buf.at[block_at(t)]
         return send(block, block, fwd_send.at[lax.div(t, 2)], a_recv.at[block_at(t)], space=sibling)
@@ -106,8 +109,7 @@
 
     for i in range(1, n_samples):
         send_b(i).start()
-    for d in range(1, chips):
-        send_a(d).start()
+    send_a(1).start()
     send_a(0).start()
 
     def start_load(t, carry):
@@ -129,6 +131,8 @@
         return carry
 
     lax.fori_loop(0, n_samples, wait_b, 0)
+    if chips > 2:
+        send_a(2).start()
     b_all = b_buf[...].reshape(n_samples * own_b, width)
     b_wide = b_all.astype(F32) * 0.5
     b_half[...] = b_wide.astype(BF16)
@@ -140,6 +144,12 @@
         @pl.when(jnp.logical_and(lax.rem(t, 2) == 1, t < n_space - 1))
         def _():
             forward(t).start()
+
+        far = lax.div(t, 2) + 3
+
+        @pl.when(jnp.logical_and(lax.rem(t, 2) == 1, far < chips))
+        def _():
+            send_far(far).start()
 
     def combine(t, odd):
         @pl.when(jnp.logical_and(odd, t >= 3))

time: 43.3 us -> 45.9 us (1.060)
  Pallas kernels: 42.5 us -> 45.1 us
    pallas_call x1, Pallas kernels: 40.8 us -> 43.3 us  [on_device(): pl.pallas_call(functools.partial(kernel, n_samples, n_space), out_shape=(...]
where the time goes in v7:
time: 45.9 us; the launch traced here: 45.7 us
  Pallas kernels  45.1 us (98%)
  between operations  0.64 us (1%)
    pallas_call x1, Pallas kernels, on_device(): pl.pallas_call(functools.partial(kernel, n_samples, n_space), out_shape=(...  43.3 us
    pallas_call x1, Pallas kernels, on_device(): pl.pallas_call(hand_over, out_shape=tuple((jax.ShapeDtypeStruct(g.shape,...  1.75 us

profile of v7, /device:TPU:0, one launch (start us, length us, event | category | flops | bytes accessed | tf_op | source)
XLA Modules:
  0.0 45.7 jit_solution(9388819497023048594)
XLA Ops:
  0.6 43.3 %cp_gradient.1 = (f32[256,256]{1,0:T(8,128)}, f32[128,256]{1,0:T(8,128)}, f32[8,256]{1,0:T(8,128)}) custom-call(bf16[8,2048,512]{2,1,0:T(8,128)(2,1)} %target.1, bf16[256,256]{1,0:T(8,128)(2,1)} %a_own.1, bf16[128,256]{1,0:T(8,128)(2,1)} %b_own.1, bf16[8,256]{1,0:T(8,128)(2,1)} %c_ref.1), custom_call_target="tpu_custom_call" | custom-call | flops 12884901888 | bytes 16777216 | tf_op jit(solution)/shard_map/cp_gradient/pallas_call | solution.py:285
  44.0 1.8 %hand_over.1 = (f32[256,256]{1,0:T(8,128)}, f32[128,256]{1,0:T(8,128)}, f32[8,256]{1,0:T(8,128)}) custom-call(f32[256,256]{1,0:T(8,128)} %get-tuple-element.6.in_a, f32[128,256]{1,0:T(8,128)} %get-tuple-element.7.in_b, f32[8,256]{1,0:T(8,128)} %get-tuple-element.8.in_c), custom_call_target="tpu_custom_call" | custom-call | tf_op jit(solution)/shard_map/hand_over/pallas_call | solution.py:329
